TPU v7x, 32 devices: a whole 2x2x4 slice. The times are simulated.
32 devices in a mesh: pair: 2 (over core), ctx: 4 (over y, x), vocab: 4 (over z).
Axes of the slice: x: 2, y: 2, z: 4, core: 2. Of those that a mesh axis runs over, the one named last changes fastest.
Arguments:
- hidden: bfloat16 [2, 512, 8192], P('pair', 'ctx'), may hold values from -8 to 8
- head_weight: bfloat16 [8192, 8192], P(('ctx', 'vocab'), 'pair'), may hold values from -2 to 2
- labels: int32 [2, 512], P('pair'), may hold values from 0 to 8191
- token_mask: int32 [2, 512], P('pair'), may hold values 0 or 1
- other_logps: float32 [2], P('pair'), may hold values from -780300 to -780000
- ref_logps: float32 [2], P('pair'), may hold values from -781300 to -781000
Outputs:
- grad_hidden: bfloat16 [2, 512, 8192], P(None, 'ctx', ('pair', 'vocab'))
- grad_head: bfloat16 [8192, 8192], P(('ctx', 'vocab'), 'pair')
All inputs are finite; a program needn't handle non-finite values. No bound on the sum of `token_mask` on one device may be relied on, other than what follows from the above.
Results may differ from a plain program's by a relative error of at most 0.012.
Values may be sent and summed in bfloat16 or wider, within the bound.
A program may use at most 128 MiB of HBM per device.

v0:
```python
import jax
import jax.numpy as jnp
from jax import lax
from jax.sharding import PartitionSpec as P

beta_value = 0.01
z_weight = 0.0001
loss_scale = 4096.0


def from_partner(block, axis, stride):
    count = lax.axis_size(axis)
    route = []
    for low in range(count):
        high = low | 1 << stride
        if high != low and high < count:
            route += [(low, high), (high, low)]
    return lax.ppermute(block, axis, route)


def local(hidden, head_weight, labels, token_mask, other_logps, ref_logps):
    pair_index = lax.axis_index("pair")
    width = hidden.shape[2]
    half_width = width // 2
    own_piece = lax.dynamic_slice_in_dim(hidden[0], pair_index * half_width, half_width, 1)
    sent_piece = lax.dynamic_slice_in_dim(hidden[0], (1 - pair_index) * half_width, half_width, 1)
    partner_piece = from_partner(sent_piece, "pair", 0)
    both_local = jnp.where(
        pair_index == 0,
        jnp.stack([own_piece, partner_piece]),
        jnp.stack([partner_piece, own_piece]),
    )
    both_rows = lax.all_gather(both_local, "ctx", axis=1, tiled=True)
    partial_logits = jnp.einsum(
        "std,vd->stv", both_rows, head_weight, preferred_element_type=jnp.float32
    )
    logits = lax.psum_scatter(partial_logits, "pair", scatter_dimension=0, tiled=True)[0]
    vocab_rows = head_weight.shape[0]
    n_ctx = lax.axis_size("ctx")
    n_vocab = lax.axis_size("vocab")
    block_index = lax.axis_index("ctx") * n_vocab + lax.axis_index("vocab")
    columns = block_index * vocab_rows + jnp.arange(vocab_rows, dtype=jnp.int32)
    onehot = (labels[0][:, None] == columns[None, :]).astype(jnp.float32)
    local_max = jnp.max(logits, axis=1)
    local_label = jnp.sum(onehot * logits, axis=1)
    row_max = lax.pmax(local_max, ("ctx", "vocab"))
    local_sum = jnp.sum(jnp.exp(logits - row_max[:, None]), axis=1)
    total_sum, label_logit = lax.psum((local_sum, local_label), ("ctx", "vocab"))
    log_total = row_max + jnp.log(total_sum)
    maskf = token_mask[0].astype(jnp.float32)
    slice_sum = jnp.sum(maskf * (label_logit - log_total))
    relative = slice_sum + other_logps[0] - ref_logps[0]
    partner = from_partner(relative, "pair", 0)
    margin = jnp.where(
        pair_index == 0, beta_value * (relative - partner), beta_value * (partner - relative)
    )
    coef = beta_value * jax.nn.sigmoid(-margin)
    seq_coef = jnp.where(pair_index == 0, -coef, coef)
    probs = jnp.exp(logits - log_total[:, None])
    logit_grad = (
        loss_scale
        * maskf[:, None]
        * (seq_coef * (onehot - probs) + 2.0 * z_weight * log_total[:, None] * probs)
    ).astype(jnp.bfloat16)
    both_grads = lax.all_gather(logit_grad[None], "pair", axis=0, tiled=True)
    grad_head = lax.dot_general(
        both_grads, both_rows, (((0, 1), (0, 1)), ((), ())), preferred_element_type=jnp.float32
    ).astype(jnp.bfloat16)
    hidden_terms = jnp.einsum(
        "stv,vd->std", both_grads, head_weight, preferred_element_type=jnp.float32
    )
    tok_rows = hidden_terms.shape[1]
    tok_local = tok_rows // n_ctx
    piece_width = half_width // n_vocab
    reordered = (
        hidden_terms.reshape(2, n_ctx, tok_local, n_vocab, piece_width)
        .transpose(1, 3, 0, 2, 4)
        .reshape(n_ctx * n_vocab * 2, tok_local, piece_width)
    )
    hidden_share = lax.psum_scatter(reordered, ("ctx", "vocab"), scatter_dimension=0, tiled=True)
    grad_hidden = hidden_share.astype(jnp.bfloat16)
    return (grad_hidden, grad_head)


def solution(mesh):
    return jax.shard_map(
        local,
        mesh=mesh,
        in_specs=(
            P("pair", "ctx", None),
            P(("ctx", "vocab"), "pair"),
            P("pair", None),
            P("pair", None),
            P("pair"),
            P("pair"),
        ),
        out_specs=(P(None, "ctx", ("pair", "vocab")), P(("ctx", "vocab"), "pair")),
        check_vma=False,
    )
```

profile of v0, /device:TPU:0, one launch (start us, length us, event | category | flops | bytes accessed | tf_op | source)
XLA Modules:
  0.0 630.1 jit_solution(10179084493092798733)
XLA Ops:
  7.2 0.0 all-gather.3.cloned.1.call-start
  7.2 1.7 constant_dynamic-slice_fusion
  8.9 0.5 collective-permute-start
  9.4 2.3 collective-permute-done
  11.7 1.6 maximum_select_fusion
  13.3 0.0 all-gather.3.cloned.1.call-update
  13.4 0.0 copy-start.1
  13.4 0.0 copy-start
  13.4 0.0 reduce-scatter.3.cloned.1.call-start
  13.4 90.3 %all-gather.3.cloned.1.call-done = bf16[2,512,4096]{2,1,0:T(8,128)(2,1)} async-done(((bf16[2,128,4096]{2,1,0:T(8,128)(2,1)}), bf16[2,512,4096]{2,1,0:T(8,128)(2,1)}) %all-gather.3.cloned.1.call-update) | async-done | bytes 8388624 | tf_op jit(solution)/shard_map/all_gather | solution.py:33
  103.8 10.4 %fusion.2 = f32[2,512,512]{2,1,0:T(8,128)} fusion(bf16[2,512,4096]{2,1,0:T(8,128)(2,1)} %all-gather.3.cloned.1.call-done, bf16[512,4096]{1,0:T(8,128)(2,1)} %param.7), kind=kOutput, calls=%fused_computation.3 | convolution fusion | flops 4294967296 | bytes 14680064 | tf_op jit(solution)/shard_map/std,vd->stv/dot_general | solution.py:34
  114.2 0.0 reduce-scatter.3.cloned.1.call-update
  114.2 0.0 all-gather.5.cloned.1.call-start
  115.5 0.0 copy-done.1
  115.6 8.4 %reduce-scatter.3.cloned.1.call-done = f32[1,512,512]{2,1,0:T(8,128)} async-done(((f32[2,512,512]{2,1,0:T(8,128)}), f32[1,512,512]{2,1,0:T(8,128)}) %reduce-scatter.3.cloned.1.call-update) | async-done | bytes 1048592 | tf_op jit(solution)/shard_map/reduce_scatter | solution.py:37
  124.0 1.4 reduce_max.9
  125.3 42.1 %pmax.7 = f32[512]{0:T(512)S(1)} all-reduce(f32[512]{0:T(512)S(1)} %reduce_max.9), channel_id=1, replica_groups=mesh['pair'=2,'ctx'=4,'vocab'=4] {'ctx','vocab'}, use_global_device_ids=true, to_apply=%region_4.5 | all-reduce | flops 512 | bytes 4096 | tf_op jit(solution)/shard_map/pmax | solution.py:46
  167.5 0.0 copy-done
  167.5 1.6 fusion.4
  169.1 36.8 %all-reduce = (f32[512]{0:T(512)S(1)}, f32[512]{0:T(512)S(1)}) all-reduce(f32[512]{0:T(512)S(1)} %get-tuple-element.3, f32[512]{0:T(512)S(1)} %get-tuple-element.2), channel_id=1, replica_groups=mesh['pair'=2,'ctx'=4,'vocab'=4] {'ctx','vocab'}, use_global_device_ids=true, to_apply=%region_6.7 | all-reduce | flops 1024 | bytes 8192 | tf_op jit(solution)/shard_map/psum | solution.py:48
  205.9 0.6 multiply_reduce_fusion
  207.1 0.9 collective-permute-start.1
  208.0 0.3 collective-permute-done.1
  209.8 2.5 multiply_convert_fusion
  212.2 0.0 all-gather.5.cloned.1.call-update
  212.3 0.2 reduce-scatter.5.cloned.1.call-start
  212.5 6.7 %all-gather.5.cloned.1.call-done = bf16[2,512,512]{2,1,0:T(8,128)(2,1)} async-done(((bf16[1,512,512]{2,1,0:T(8,128)(2,1)}), bf16[2,512,512]{2,1,0:T(8,128)(2,1)}) %all-gather.5.cloned.1.call-update) | async-done | bytes 1048592 | tf_op jit(solution)/shard_map/all_gather | solution.py:65
  219.2 12.7 %fusion = f32[2,512,4096]{2,1,0:T(8,128)} fusion(bf16[2,512,512]{2,1,0:T(8,128)(2,1)} %all-gather.5.cloned.1.call-done, bf16[512,4096]{1,0:T(8,128)(2,1)} %param.7), kind=kOutput, calls=%fused_computation.1 | convolution fusion | flops 4294967296 | bytes 22020096 | tf_op jit(solution)/shard_map/stv,vd->std/dot_general | solution.py:69
  232.0 20.4 %reshape.98 = f32[2,4,128,4,1024]{4,3,2,1,0:T(4,128)} reshape(f32[2,512,4096]{2,1,0:T(8,128)} %fusion) | data formatting | bytes 33554432 | tf_op jit(solution)/shard_map/reshape | solution.py:76
  252.4 17.7 %copy.10 = f32[4,4,2,128,1024]{4,3,2,1,0:T(8,128)} copy(f32[4,4,2,128,1024]{4,1,3,0,2:T(4,128)} %bitcast.32) | data formatting | bytes 33554432 | tf_op jit(solution)/shard_map/transpose | solution.py:77
  270.1 0.0 copy-start.2
  270.1 0.0 reduce-scatter.5.cloned.1.call-update
  270.1 1.2 copy-done.2
  271.3 9.5 %bitcast_convert_fusion = bf16[512,4096]{1,0:T(8,128)(2,1)} fusion(bf16[2,512,512]{2,1,0:T(8,128)(2,1)S(1)} %copy-done.2, bf16[2,512,4096]{2,1,0:T(8,128)(2,1)} %all-gather.3.cloned.1.call-done), kind=kOutput, calls=%fused_computation | convolution fusion | flops 4297064448 | bytes 13631488 | tf_op jit(solution)/shard_map/dot_general | solution.py:66
  280.8 340.7 %reduce-scatter.5.cloned.1.call-done = f32[2,128,1024]{2,1,0:T(8,128)} async-done(((f32[32,128,1024]{2,1,0:T(8,128)}), f32[2,128,1024]{2,1,0:T(8,128)}) %reduce-scatter.5.cloned.1.call-update) | async-done | bytes 1048592 | tf_op jit(solution)/shard_map/reduce_scatter | solution.py:80
  621.5 2.1 convert_element_type.34
  (3 shorter events, 0.0 us)
Async XLA Ops:
  7.2 96.6 %all-gather.3.cloned.1.call-start = ((), (), s32[]{:S(2)}) async-start(), calls=%async_computation.2 | async-start | bytes 10485760 | tf_op jit(solution)/shard_map/all_gather | solution.py:33
  8.9 2.8 collective-permute-start
  13.4 102.2 %copy-start.1 = (s32[1,512]{1,0:T(1,128)S(1)}, s32[1,512]{1,0:T(1,128)}, u32[]{:S(2)}) copy-start(s32[1,512]{1,0:T(1,128)} %param.9) | copy-start | bytes 6148
  13.4 154.1 %copy-start = (s32[1,512]{1,0:T(1,128)S(1)}, s32[1,512]{1,0:T(1,128)}, u32[]{:S(2)}) copy-start(s32[1,512]{1,0:T(1,128)} %param.8) | copy-start | bytes 6148
  13.4 110.6 %reduce-scatter.3.cloned.1.call-start = ((), (), s32[]{:S(2)}) async-start(), calls=%async_computation.3 | async-start | bytes 3145728 | tf_op jit(solution)/shard_map/reduce_scatter | solution.py:37
  114.2 105.0 %all-gather.5.cloned.1.call-start = ((), (), s32[]{:S(2)}) async-start(), calls=%async_computation.4 | async-start | bytes 1572864 | tf_op jit(solution)/shard_map/all_gather | solution.py:65
  207.1 1.2 collective-permute-start.1
  212.3 409.2 %reduce-scatter.5.cloned.1.call-start = ((), (), s32[]{:S(2)}) async-start(), calls=%async_computation.5 | async-start | bytes 17825792 | tf_op jit(solution)/shard_map/reduce_scatter | solution.py:80
  270.1 1.2 copy-start.2
Sparse Core Ops, SparseCore 0:
  13.5 90.2 all-gather.2
  114.3 9.6 reduce-scatter.2
  212.4 6.7 all-gather.4
  270.2 351.2 reduce-scatter.4
where the time goes:
time: 631 us; the launch traced here: 630 us
  waiting for transfers between devices  449 us (71%)
  blocking collectives  78.9 us (13%)
  local copies, waits for them, and re-layouts  41 us (6%)
  matrix products  32.6 us (5%)
  between operations  17.3 us (3%)
  other arithmetic  9.83 us (2%)
    reduce_scatter x1, waiting for transfers between devices, local(): lax.psum_scatter(reordered, ('ctx', 'vocab'), scatter_dimension=0, tiled=...  341 us
    all_gather x1, waiting for transfers between devices, local(): both_rows = lax.all_gather(both_local, 'ctx', axis=1, tiled=True)  90.3 us
    pmax x1, blocking collectives, local(): row_max = lax.pmax(local_max, ('ctx', 'vocab'))  42.1 us
    psum x1, blocking collectives, local(): lax.psum((local_sum, local_label), ('ctx', 'vocab'))  36.8 us
    reshape x1, local copies, waits for them, and re-layouts, local(): hidden_terms.reshape(2, n_ctx, tok_local, n_vocab, piece_width)  20.4 us
    transpose x1, local copies, waits for them, and re-layouts, local(): reordered = hidden_terms.reshape(2, n_ctx, tok_local, n_vocab, piece_widt...  17.7 us
    dot_general x1, matrix products, local(): jnp.einsum('stv,vd->std', both_grads, head_weight, preferred_element_type...  12.7 us
  transfers between devices with their start and end apart: 6, of which 6 were waited for; matrix products, arithmetic and copies ran while one was open for 2% of the time, Pallas kernels for 0%

commit v1 on v0

v1 whole, which is shorter than its diff:
```python
import functools

import jax
import jax.numpy as jnp
from jax import lax
from jax.experimental import pallas as pl
from jax.experimental.pallas import tpu as pltpu
from jax.sharding import PartitionSpec as P

beta_value = 0.01
z_weight = 0.0001
loss_scale = 4096.0
F32, BF16 = jnp.float32, jnp.bfloat16
PARTS = 4


def flip(index, mask):
    bit = 1
    while bit <= mask:
        if mask & bit:
            index = index + bit * (1 - 2 * lax.rem(lax.div(index, bit), 2))
        bit *= 2
    return index


def kernel(
    n, hid, w_hbm, lab_in, msk_in, oth_in, ref_in, gh_out, head_out,
    w, H, LT, LR, GT, G, S1, R1, S2, R2, ZS, ZR, FA, HO, GO, st, st2, zst, cst, auxi, auxf,
    lsem, psem, aux_sem, ag_s, ag_r, lt_s, lt_r, zst_s, zst_r, cst_s, cst_r,
    s1_s, s1_r, s2_s, s2_r, z_s, z_r, ho_sem,
):
    p, c, z = lax.axis_index("pair"), lax.axis_index("ctx"), lax.axis_index("vocab")
    q = 1 - p
    partner = (q, c, z)
    tl = H.shape[2]
    half = w.shape[1]
    rows = w.shape[0]
    m = n // PARTS
    cw = half // n
    CW = half // PARTS
    ktile = 512

    def at_ctx(d):
        return (p, flip(c, d), z)

    def at_vocab(x):
        return (p, c, flip(z, x))

    def remote(src, dst, ss, rs, dev):
        return pltpu.make_async_remote_copy(
            src_ref=src, dst_ref=dst, send_sem=ss, recv_sem=rs,
            device_id=dev, device_id_type=pl.DeviceIdType.MESH,
        )

    cp_w = pltpu.make_async_copy(w_hbm, w, lsem.at[0])
    cp_w.start()
    own_cols = pl.ds(pl.multiple_of(p * half, half), half)
    other_cols = pl.ds(pl.multiple_of(q * half, half), half)
    cp_h = pltpu.make_async_copy(hid.at[0, :, own_cols], H.at[0, p], lsem.at[1])
    cp_h.start()
    auxi[p, 0:1, :] = lab_in[...]
    auxi[p, 1:2, :] = msk_in[...]
    auxf[p, 0:1, :] = jnp.broadcast_to(oth_in[...], (1, 128))
    auxf[p, 1:2, :] = jnp.broadcast_to(ref_in[...], (1, 128))

    barrier = pltpu.get_barrier_semaphore()
    peers = [partner] + [at_ctx(d) for d in (1, 2, 3)] + [at_vocab(x) for x in range(1, n)]
    for dev in peers:
        pl.semaphore_signal(barrier, inc=1, device_id=dev, device_id_type=pl.DeviceIdType.MESH)
    pl.semaphore_wait(barrier, len(peers))

    to_partner = remote(hid.at[0, :, other_cols], H.at[0, p], psem.at[0], psem.at[1], partner)
    to_partner.start()
    ag = []
    for d in (1, 2):
        cp = remote(hid.at[0, :, own_cols], H.at[d, p], ag_s.at[d, p], ag_r.at[d, p], at_ctx(d))
        cp.start()
        ag.append(cp)
    ax = [
        remote(auxi.at[p], auxi.at[p], aux_sem.at[0], aux_sem.at[1], partner),
        remote(auxf.at[p], auxf.at[p], aux_sem.at[2], aux_sem.at[3], partner),
    ]
    for cp in ax:
        cp.start()
    to_partner.wait_recv()
    for d in (1, 2):
        cp = remote(H.at[0, q], H.at[d, q], ag_s.at[d, q], ag_r.at[d, q], at_ctx(d))
        cp.start()
        ag.append(cp)
    cp_w.wait()
    cp_h.wait()

    def ag_wait(d, s):
        remote(H.at[d, s], H.at[d, s], ag_s.at[d, s], ag_r.at[d, s], at_ctx(d)).wait_recv()

    lt_copies = []

    def logits(d):
        LT[d] = jnp.zeros((rows, 2 * tl), F32)

        def body(k, carry):
            cols = pl.ds(pl.multiple_of(k * ktile, ktile), ktile)
            block = H[d, :, :, cols].reshape(2 * tl, ktile)
            LT[d] += lax.dot_general(
                w[:, cols], block, (((1,), (1,)), ((), ())), preferred_element_type=F32
            )
            return carry

        lax.fori_loop(0, half // ktile, body, 0)
        cp = remote(LT.at[d], LR.at[d], lt_s.at[d], lt_r.at[d], partner)
        cp.start()
        lt_copies.append(cp)

    base = (c * n + z) * rows

    def is_label(d, s):
        toks = pl.ds(pl.multiple_of(flip(c, d) * tl, tl), tl)
        return lax.broadcasted_iota(jnp.int32, (rows, tl), 0) == auxi[s, 0:1, toks] - base

    def local_stats(d):
        lt_copies[d].wait()
        for s in range(2):
            lanes = slice(s * tl, (s + 1) * tl)
            l = LT[d, :, lanes] + LR[d, :, lanes]
            top = jnp.max(l, axis=0, keepdims=True)
            e = jnp.exp(l - top)
            LT[d, :, lanes] = e
            st[d, s, 0:1, :] = top
            st[d, s, 1:2, :] = jnp.sum(e, axis=0, keepdims=True)
            st[d, s, 2:3, :] = jnp.sum(jnp.where(is_label(d, s), l, 0.0), axis=0, keepdims=True)

    logits(0)
    ag_wait(1, 0)
    fwd0 = remote(H.at[1, 0], H.at[3, 0], ag_s.at[3, 0], ag_r.at[3, 0], at_ctx(2))
    fwd0.start()
    ag_wait(2, 1)
    fwd1 = remote(H.at[2, 1], H.at[3, 1], ag_s.at[3, 1], ag_r.at[3, 1], at_ctx(1))
    fwd1.start()
    for cp in ax:
        cp.wait()
    ag_wait(1, 1)
    logits(1)
    ag_wait(2, 0)
    logits(2)
    local_stats(0)
    local_stats(1)
    local_stats(2)
    ag_wait(3, 0)
    ag_wait(3, 1)
    logits(3)
    local_stats(3)

    zc = []
    for x in range(1, n):
        cp = remote(st, zst.at[x], zst_s.at[x], zst_r.at[x], at_vocab(x))
        cp.start()
        zc.append(cp)
    for cp in zc:
        cp.wait()

    def merge(parts):
        top = functools.reduce(jnp.maximum, [t for t, _, _ in parts])
        total = sum(s * jnp.exp(t - top) for t, s, _ in parts)
        label = sum(l for _, _, l in parts)
        return top, total, label

    def read(ref, *at):
        return tuple(ref[(*at, slice(r, r + 1), slice(None))] for r in range(3))

    for d in range(4):
        for s in range(2):
            got = merge([read(st, d, s)] + [read(zst, x, d, s) for x in range(1, n)])
            for r in range(3):
                st2[d, s, r : r + 1, :] = got[r]
    cc = []
    for k in (3, 1, 2):
        cp = remote(st2, cst.at[k], cst_s.at[k], cst_r.at[k], at_ctx(k))
        cp.start()
        cc.append(cp)
    for cp in cc:
        cp.wait()
    log_total, maskf = {}, {}
    relative = []
    for s in range(2):
        acc = jnp.zeros((1, tl), F32)
        for d in range(4):
            top, total, label = merge(
                [read(st2, d, s)] + [read(cst, k, k ^ d, s) for k in (1, 2, 3)]
            )
            lt = top + jnp.log(total)
            toks = pl.ds(pl.multiple_of(flip(c, d) * tl, tl), tl)
            mk = auxi[s, 1:2, toks].astype(F32)
            log_total[d, s], maskf[d, s] = lt, mk
            acc = acc + mk * (label - lt)
        slice_sum = jnp.sum(acc, axis=1, keepdims=True)
        relative.append((slice_sum + auxf[s, 0:1, 0:1]) - auxf[s, 1:2, 0:1])
    margin = beta_value * (relative[0] - relative[1])
    coef = beta_value / (1.0 + jnp.exp(margin))

    for d in (3, 1, 2, 0):
        for s in range(2):
            seq = coef if s == 1 else -coef
            lanes = slice(s * tl, (s + 1) * tl)
            lt, mk = log_total[d, s], maskf[d, s]
            b = loss_scale * mk * seq
            a = loss_scale * mk * (2.0 * z_weight * lt - seq) * jnp.exp(st[d, s, 0:1, :] - lt)
            g = LT[d, :, lanes] * a + jnp.where(is_label(d, s), b, 0.0)
            GT[d, :, lanes] = g.astype(BF16)
            G[d, s] = g.T.astype(BF16)

    zs = lax.div(z, m)
    first, second = (1, 2), (2, 1)

    def cols(i):
        return pl.ds(pl.multiple_of(flip(zs, PARTS - 1 - i) * CW, CW), CW)

    def term(d, s, i):
        return jnp.dot(G[d, s], w[:, cols(i)], preferred_element_type=F32)

    c1, c2, cz = {}, {}, []

    def send_first(i):
        for s in range(2):
            f = first[s]
            S1[i, s, 1] = term(3, s, i).astype(BF16)
            S1[i, s, 0] = term(f, s, i).astype(BF16)
            c1[i, s] = remote(S1.at[i, s], R1.at[i, s], s1_s.at[i, s], s1_r.at[i, s], at_ctx(f))
            c1[i, s].start()

    def send_second(i):
        for s in range(2):
            g = second[s]
            mine = term(g, s, i)
            c1[i, s].wait_recv()
            S2[i, s] = (mine + R1[i, s, 1].astype(F32)).astype(BF16)
            c2[i, s] = remote(S2.at[i, s], R2.at[i, s], s2_s.at[i, s], s2_r.at[i, s], at_ctx(g))
            c2[i, s].start()

    def send_vocab(i):
        for s in range(2):
            mine = term(0, s, i) + R1[i, s, 0].astype(F32)
            c2[i, s].wait_recv()
            mine = mine + R2[i, s].astype(F32)
            if i == PARTS - 1:
                FA[s] = mine
            ZS[i, s] = mine.astype(BF16)
        zm = lax.rem(z, m)
        for k in reversed(range(m)):
            x = (PARTS - 1 - i) * m + k
            if x == 0:
                continue
            if m == 1:
                src = ZS.at[i]
            else:
                src = ZS.at[i, :, :, pl.ds(pl.multiple_of(flip(zm, k) * cw, cw), cw)]
            cp = remote(src, ZR.at[x], z_s.at[x], z_r.at[x], at_vocab(x))
            cp.start()
            cz.append(cp)

    tile = 512
    head_tiles = half // tile

    def head_copy(t):
        where = pl.ds(pl.multiple_of(t * tile, tile), tile)
        return pltpu.make_async_copy(HO.at[:, where], head_out.at[:, where], ho_sem.at[t])

    def head(low, high):
        def body(t, carry):
            where = pl.ds(pl.multiple_of(t * tile, tile), tile)
            acc = jnp.zeros((rows, tile), F32)
            for d in range(4):
                acc += jnp.dot(
                    GT[d], H[d, :, :, where].reshape(2 * tl, tile), preferred_element_type=F32
                )
            HO[:, where] = acc.astype(BF16)
            head_copy(t).start()
            return carry

        lax.fori_loop(low, high, body, 0)

    send_first(0)
    send_first(1)
    head(0, head_tiles // 2)
    send_second(0)
    send_first(2)
    head(head_tiles // 2, head_tiles)
    send_second(1)
    send_vocab(0)
    send_first(3)
    send_second(2)
    send_vocab(1)
    send_second(3)
    send_vocab(2)
    send_vocab(3)
    zm = lax.rem(z, m)
    own = pl.ds(0, cw) if m == 1 else pl.ds(pl.multiple_of(zm * cw, cw), cw)
    for cp in cz:
        cp.wait_recv()
    for s in range(2):
        total = FA[s, :, own]
        for x in range(1, n):
            total = total + ZR[x, s].astype(F32)
        GO[s] = total.astype(BF16)
    out = pltpu.make_async_copy(GO, gh_out, lsem.at[2])
    out.start()
    to_partner.wait_send()
    for cp in ag + [fwd0, fwd1]:
        cp.wait_send()
    for cp in list(c1.values()) + list(c2.values()) + cz:
        cp.wait_send()

    def drain(t, carry):
        head_copy(t).wait()
        return carry

    lax.fori_loop(0, head_tiles, drain, 0)
    out.wait()


def solution(mesh):
    n = mesh.shape["vocab"]

    def local(hidden, head_weight, labels, token_mask, other_logps, ref_logps):
        tl = hidden.shape[1]
        rows, half = head_weight.shape
        toks = labels.shape[1]
        CW, cw = half // PARTS, half // n
        vm = pltpu.VMEM
        dma = pltpu.SemaphoreType.DMA
        any_spec = pl.BlockSpec(memory_space=pl.ANY)
        vmem_spec = pl.BlockSpec(memory_space=pltpu.VMEM)
        return pl.pallas_call(
            functools.partial(kernel, n),
            out_shape=(
                jax.ShapeDtypeStruct((2, tl, cw), BF16),
                jax.ShapeDtypeStruct((rows, half), BF16),
            ),
            in_specs=[any_spec, any_spec] + [vmem_spec] * 4,
            out_specs=(any_spec, any_spec),
            scratch_shapes=[
                vm((rows, half), BF16),
                vm((4, 2, tl, half), BF16),
                vm((4, rows, 2 * tl), F32),
                vm((4, rows, 2 * tl), F32),
                vm((4, rows, 2 * tl), BF16),
                vm((4, 2, tl, rows), BF16),
                vm((PARTS, 2, 2, tl, CW), BF16),
                vm((PARTS, 2, 2, tl, CW), BF16),
                vm((PARTS, 2, tl, CW), BF16),
                vm((PARTS, 2, tl, CW), BF16),
                vm((PARTS, 2, tl, CW), BF16),
                vm((n, 2, tl, cw), BF16),
                vm((2, tl, CW), F32),
                vm((rows, half), BF16),
                vm((2, tl, cw), BF16),
                vm((4, 2, 8, tl), F32),
                vm((4, 2, 8, tl), F32),
                vm((n, 4, 2, 8, tl), F32),
                vm((4, 4, 2, 8, tl), F32),
                vm((2, 8, toks), jnp.int32),
                vm((2, 8, 128), F32),
                dma((3,)),
                dma((2,)),
                dma((4,)),
                dma((4, 2)),
                dma((4, 2)),
                dma((4,)),
                dma((4,)),
                dma((n,)),
                dma((n,)),
                dma((4,)),
                dma((4,)),
                dma((PARTS, 2)),
                dma((PARTS, 2)),
                dma((PARTS, 2)),
                dma((PARTS, 2)),
                dma((n,)),
                dma((n,)),
                dma((half // 512,)),
            ],
            compiler_params=pltpu.CompilerParams(
                collective_id=0, has_side_effects=True, vmem_limit_bytes=58 * 1024 * 1024
            ),
            cost_estimate=pl.CostEstimate(
                flops=6 * 8 * tl * rows * half, bytes_accessed=6 * rows * half, transcendentals=0
            ),
        )(
            hidden, head_weight, labels, token_mask,
            other_logps.reshape(1, 1), ref_logps.reshape(1, 1),
        )

    return jax.shard_map(
        local,
        mesh=mesh,
        in_specs=(
            P("pair", "ctx", None),
            P(("ctx", "vocab"), "pair"),
            P("pair", None),
            P("pair", None),
            P("pair"),
            P("pair"),
        ),
        out_specs=(P(None, "ctx", ("pair", "vocab")), P(("ctx", "vocab"), "pair")),
        check_vma=False,
    )
```

time: 631 us -> 185 us (0.29)
  waiting for transfers between devices: 449 us -> 0 us
  Pallas kernels: 0 us -> 177 us
  blocking collectives: 78.9 us -> 0 us
  local copies, waits for them, and re-layouts: 41 us -> 6.57 us
  matrix products: 32.6 us -> 0 us
  between operations: 17.3 us -> 1.93 us
  other arithmetic: 9.83 us -> 0 us
    reduce_scatter x2 -> x0, waiting for transfers between devices: 349 us -> none  [the longest x1 341 us: local(): lax.psum_scatter(reordered, ('ctx', 'vocab'), scatter_dimension=0, tiled=...]
    pallas_call x0 -> x1, Pallas kernels: none -> 177 us  [local(): pl.pallas_call(functools.partial(kernel, n), out_shape=(jax.ShapeDtypeStr...]
    all_gather x2 -> x0, waiting for transfers between devices: 97 us -> none  [the longest x1 90.3 us: local(): both_rows = lax.all_gather(both_local, 'ctx', axis=1, tiled=True)]
    pmax x1 -> x0, blocking collectives: 42.1 us -> none  [local(): row_max = lax.pmax(local_max, ('ctx', 'vocab'))]
    psum x1 -> x0, blocking collectives: 36.8 us -> none  [local(): lax.psum((local_sum, local_label), ('ctx', 'vocab'))]
    dot_general x3 -> x0, matrix products: 32.6 us -> none  [the longest x1 12.7 us: local(): jnp.einsum('stv,vd->std', both_grads, head_weight, preferred_element_type...]
    reshape x1 -> x0, local copies, waits for them, and re-layouts: 20.4 us -> none  [local(): hidden_terms.reshape(2, n_ctx, tok_local, n_vocab, piece_width)]
    transpose x1 -> x0, local copies, waits for them, and re-layouts: 17.7 us -> none  [local(): reordered = hidden_terms.reshape(2, n_ctx, tok_local, n_vocab, piece_widt...]
  transfers between devices with their start and end apart: 6 -> 0, of which waited for: 6 -> 0; matrix products, arithmetic and copies ran while one was open for 2% -> 0% of each run, Pallas kernels for 0% -> 0%
where the time goes in v1:
time: 185 us
  Pallas kernels  177 us (96%)
  local copies, waits for them, and re-layouts  6.57 us (4%)
  between operations  1.93 us (1%)
    pallas_call x1, Pallas kernels, local(): pl.pallas_call(functools.partial(kernel, n), out_shape=(jax.ShapeDtypeStr...  177 us
    unnamed x2, local copies, waits for them, and re-layouts  6.57 us

profile of v1, /device:TPU:0, one launch (start us, length us, event | category | flops | bytes accessed | tf_op | source)
XLA Modules:
  0.0 185.0 jit_solution(13889558577813489157)
XLA Ops:
  1.9 176.5 %shard_map.77 = (bf16[2,128,1024]{2,1,0:T(8,128)(2,1)}, bf16[512,4096]{1,0:T(8,128)(2,1)}) custom-call(bf16[1,128,8192]{2,1,0:T(8,128)(2,1)} %hid.1, bf16[512,4096]{1,0:T(8,128)(2,1)} %w_hbm.1, s32[1,512]{1,0:T(1,128)} %lab_in.1, s32[1,512]{1,0:T(1,128)} %msk_in.1, f32[1,1]{1,0:T(1,128)} %bitcast.2.oth_in, f32[1,1]{1,0:T(1,128)} %bitcast.3.ref_in), custom_call_target="tpu_custom_call" | custom-call | flops 12884901888 | bytes 12582912 | tf_op jit(solution)/shard_map/pallas_call | solution.py:332
  178.4 1.9 %copy.12 = bf16[2,128,1024]{2,1,0:T(8,128)(2,1)} copy(bf16[2,128,1024]{2,1,0:T(8,128)(2,1)} %get-tuple-element.4) | data formatting | bytes 1048576
  180.3 4.7 %copy.13 = bf16[512,4096]{1,0:T(8,128)(2,1)} copy(bf16[512,4096]{1,0:T(8,128)(2,1)} %get-tuple-element.5) | data formatting | bytes 8388608

commit v2 on v1

--- a/solution.py
+++ b/solution.py
@@ -25,8 +25,8 @@
 
 def kernel(
     n, hid, w_hbm, lab_in, msk_in, oth_in, ref_in, gh_out, head_out,
-    w, H, LT, LR, GT, G, S1, R1, S2, R2, ZS, ZR, FA, HO, GO, st, st2, zst, cst, auxi, auxf,
-    lsem, psem, aux_sem, ag_s, ag_r, lt_s, lt_r, zst_s, zst_r, cst_s, cst_r,
+    w, H, LT, LR, GT, G, S1, R1, S2, R2, ZS, ZR, FA, HO, GO, st, st2, zst, cst, ab, auxi, auxf,
+    lsem, psem, aux_sem, az_s, az_r, ag_s, ag_r, ch_s, ch_r, lt_s, lt_r, zst_s, zst_r, cst_s, cst_r,
     s1_s, s1_r, s2_s, s2_r, z_s, z_r, ho_sem,
 ):
     p, c, z = lax.axis_index("pair"), lax.axis_index("ctx"), lax.axis_index("vocab")
@@ -39,6 +39,10 @@
     cw = half // n
     CW = half // PARTS
     ktile = 512
+    zs = lax.div(z, m)
+    zq = half * 3 // (8 * PARTS)
+    rest = slice(zq * PARTS, half)
+    hr = tl // 2
 
     def at_ctx(d):
         return (p, flip(c, d), z)
@@ -72,10 +76,35 @@
     to_partner = remote(hid.at[0, :, other_cols], H.at[0, p], psem.at[0], psem.at[1], partner)
     to_partner.start()
     ag = []
-    for d in (1, 2):
-        cp = remote(hid.at[0, :, own_cols], H.at[d, p], ag_s.at[d, p], ag_r.at[d, p], at_ctx(d))
+
+    def zcols(k):
+        return pl.ds(pl.multiple_of(k * zq, zq), zq)
+
+    def send_z(d, s, src, to, into):
+        cp = remote(src, H.at[into, s, :, zcols(zs)], az_s.at[into, s], az_r.at[into, s], at_ctx(to))
         cp.start()
         ag.append(cp)
+
+    def send_rest(h, s, src, to, into):
+        cp = remote(
+            src, H.at[into, s, h * hr : (h + 1) * hr, rest],
+            ag_s.at[into, s, h], ag_r.at[into, s, h], at_ctx(to),
+        )
+        cp.start()
+        ag.append(cp)
+
+    def own_rest(h):
+        where = pl.ds(pl.multiple_of(p * half + zq * PARTS, 128), half - zq * PARTS)
+        return hid.at[0, h * hr : (h + 1) * hr, where]
+
+    def held_rest(d, s, h):
+        return H.at[d, s, h * hr : (h + 1) * hr, rest]
+
+    own_z = hid.at[0, :, pl.ds(pl.multiple_of(p * half + zs * zq, 128), zq)]
+    for d in (1, 2):
+        send_z(0, p, own_z, d, d)
+    for d in (1, 2):
+        send_rest(0, p, own_rest(0), d, d)
     ax = [
         remote(auxi.at[p], auxi.at[p], aux_sem.at[0], aux_sem.at[1], partner),
         remote(auxf.at[p], auxf.at[p], aux_sem.at[2], aux_sem.at[3], partner),
@@ -84,14 +113,68 @@
         cp.start()
     to_partner.wait_recv()
     for d in (1, 2):
-        cp = remote(H.at[0, q], H.at[d, q], ag_s.at[d, q], ag_r.at[d, q], at_ctx(d))
-        cp.start()
-        ag.append(cp)
+        send_z(0, q, H.at[0, q, :, zcols(zs)], d, d)
+    for d in (1, 2):
+        send_rest(1, p, own_rest(1), d, d)
+
+    def z_wait(d, s):
+        part = H.at[d, s, :, zcols(zs)]
+        remote(part, part, az_s.at[d, s], az_r.at[d, s], at_ctx(d)).wait_recv()
+
+    def rest_wait(d, s):
+        for h in range(2):
+            part = held_rest(d, s, h)
+            remote(part, part, ag_s.at[d, s, h], ag_r.at[d, s, h], at_ctx(d)).wait_recv()
+
+    def chain_copy(way, j, d, part):
+        piece = H.at[d, :, :, zcols(part)]
+        dev = (p, c, lax.rem(z + n + (m if way == 0 else -m), n))
+        return remote(piece, piece, ch_s.at[way, j, d], ch_r.at[way, j, d], dev)
+
+    def chain_sent(way, j):
+        part = zs - j if way == 0 else zs + j
+        if way == 0:
+            return part, jnp.logical_and(zs < PARTS - 1, part >= 0)
+        return part, jnp.logical_and(zs > 0, part < PARTS)
+
+    def chain_send(j, blocks):
+        for d in blocks:
+            for way in range(2):
+                part, there = chain_sent(way, j)
+
+                @pl.when(there)
+                def _():
+                    chain_copy(way, j, d, part).start()
+
+    def chain_wait_send(j, d):
+        for way in range(2):
+            part, there = chain_sent(way, j)
+
+            @pl.when(there)
+            def _():
+                chain_copy(way, j, d, part).wait_send()
+
+    def chain_recv(j, blocks):
+        for d in blocks:
+            for way in range(2):
+                part = zs - 1 - j if way == 0 else zs + 1 + j
+
+                @pl.when(part >= 0 if way == 0 else part < PARTS)
+                def _():
+                    chain_copy(way, j, d, part).wait_recv()
+
+    z_wait(1, 0)
+    send_z(1, 0, H.at[1, 0, :, zcols(zs)], 2, 3)
+    z_wait(2, 1)
+    send_z(2, 1, H.at[2, 1, :, zcols(zs)], 1, 3)
+    for h in range(2):
+        for d in (1, 2):
+            send_rest(h, q, held_rest(0, q, h), d, d)
+    z_wait(1, 1)
+    z_wait(2, 0)
+    chain_send(0, (1, 2))
     cp_w.wait()
     cp_h.wait()
-
-    def ag_wait(d, s):
-        remote(H.at[d, s], H.at[d, s], ag_s.at[d, s], ag_r.at[d, s], at_ctx(d)).wait_recv()
 
     lt_copies = []
 
@@ -120,33 +203,49 @@
     def local_stats(d):
         lt_copies[d].wait()
         for s in range(2):
+            u = 2 * d + s
             lanes = slice(s * tl, (s + 1) * tl)
             l = LT[d, :, lanes] + LR[d, :, lanes]
             top = jnp.max(l, axis=0, keepdims=True)
             e = jnp.exp(l - top)
             LT[d, :, lanes] = e
-            st[d, s, 0:1, :] = top
-            st[d, s, 1:2, :] = jnp.sum(e, axis=0, keepdims=True)
-            st[d, s, 2:3, :] = jnp.sum(jnp.where(is_label(d, s), l, 0.0), axis=0, keepdims=True)
+            st[0, u : u + 1, :] = top
+            st[1, u : u + 1, :] = jnp.sum(e, axis=0, keepdims=True)
+            st[2, u : u + 1, :] = jnp.sum(
+                jnp.where(is_label(d, s), l, 0.0), axis=0, keepdims=True
+            )
 
     logits(0)
-    ag_wait(1, 0)
-    fwd0 = remote(H.at[1, 0], H.at[3, 0], ag_s.at[3, 0], ag_r.at[3, 0], at_ctx(2))
-    fwd0.start()
-    ag_wait(2, 1)
-    fwd1 = remote(H.at[2, 1], H.at[3, 1], ag_s.at[3, 1], ag_r.at[3, 1], at_ctx(1))
-    fwd1.start()
+    z_wait(3, 0)
+    z_wait(3, 1)
+    chain_send(0, (3,))
+    chain_recv(0, (1, 2))
+    chain_send(1, (1, 2))
+    chain_recv(0, (3,))
+    chain_send(1, (3,))
     for cp in ax:
         cp.wait()
-    ag_wait(1, 1)
+    local_stats(0)
+    chain_recv(1, (1, 2))
+    chain_send(2, (1, 2))
+    rest_wait(1, 0)
+    for h in range(2):
+        send_rest(h, 0, held_rest(1, 0, h), 2, 3)
+    rest_wait(2, 1)
+    for h in range(2):
+        send_rest(h, 1, held_rest(2, 1, h), 1, 3)
+    chain_recv(1, (3,))
+    chain_send(2, (3,))
+    rest_wait(1, 1)
+    rest_wait(2, 0)
+    chain_recv(2, (1, 2))
     logits(1)
-    ag_wait(2, 0)
     logits(2)
-    local_stats(0)
     local_stats(1)
     local_stats(2)
-    ag_wait(3, 0)
-    ag_wait(3, 1)
+    chain_recv(2, (3,))
+    rest_wait(3, 0)
+    rest_wait(3, 1)
     logits(3)
     local_stats(3)
 
@@ -165,13 +264,11 @@
         return top, total, label
 
     def read(ref, *at):
-        return tuple(ref[(*at, slice(r, r + 1), slice(None))] for r in range(3))
-
-    for d in range(4):
-        for s in range(2):
-            got = merge([read(st, d, s)] + [read(zst, x, d, s) for x in range(1, n)])
-            for r in range(3):
-                st2[d, s, r : r + 1, :] = got[r]
+        return tuple(ref[(*at, r)] for r in range(3))
+
+    got = merge([read(st)] + [read(zst, x) for x in range(1, n)])
+    for r in range(3):
+        st2[r] = got[r]
     cc = []
     for k in (3, 1, 2):
         cp = remote(st2, cst.at[k], cst_s.at[k], cst_r.at[k], at_ctx(k))
@@ -179,36 +276,43 @@
         cc.append(cp)
     for cp in cc:
         cp.wait()
-    log_total, maskf = {}, {}
+
+    def read_ctx(k):
+        return tuple(
+            jnp.concatenate(
+                [cst[k, r, 2 * (k ^ d) : 2 * (k ^ d) + 2, :] for d in range(4)], axis=0
+            )
+            for r in range(3)
+        )
+
+    top, total, label = merge([got] + [read_ctx(k) for k in (1, 2, 3)])
+    lt = top + jnp.log(total)
+    mask_rows = []
+    for d in range(4):
+        toks = pl.ds(pl.multiple_of(flip(c, d) * tl, tl), tl)
+        mask_rows += [auxi[0, 1:2, toks], auxi[1, 1:2, toks]]
+    mk = jnp.concatenate(mask_rows, axis=0).astype(F32)
+    response = lax.rem(lax.broadcasted_iota(jnp.int32, (8, tl), 0), 2)
+    counted = mk * (label - lt)
     relative = []
     for s in range(2):
-        acc = jnp.zeros((1, tl), F32)
-        for d in range(4):
-            top, total, label = merge(
-                [read(st2, d, s)] + [read(cst, k, k ^ d, s) for k in (1, 2, 3)]
-            )
-            lt = top + jnp.log(total)
-            toks = pl.ds(pl.multiple_of(flip(c, d) * tl, tl), tl)
-            mk = auxi[s, 1:2, toks].astype(F32)
-            log_total[d, s], maskf[d, s] = lt, mk
-            acc = acc + mk * (label - lt)
-        slice_sum = jnp.sum(acc, axis=1, keepdims=True)
+        part = jnp.sum(jnp.where(response == s, counted, 0.0), axis=0, keepdims=True)
+        slice_sum = jnp.sum(part, axis=1, keepdims=True)
         relative.append((slice_sum + auxf[s, 0:1, 0:1]) - auxf[s, 1:2, 0:1])
     margin = beta_value * (relative[0] - relative[1])
     coef = beta_value / (1.0 + jnp.exp(margin))
-
-    for d in (3, 1, 2, 0):
-        for s in range(2):
-            seq = coef if s == 1 else -coef
-            lanes = slice(s * tl, (s + 1) * tl)
-            lt, mk = log_total[d, s], maskf[d, s]
-            b = loss_scale * mk * seq
-            a = loss_scale * mk * (2.0 * z_weight * lt - seq) * jnp.exp(st[d, s, 0:1, :] - lt)
-            g = LT[d, :, lanes] * a + jnp.where(is_label(d, s), b, 0.0)
-            GT[d, :, lanes] = g.astype(BF16)
-            G[d, s] = g.T.astype(BF16)
-
-    zs = lax.div(z, m)
+    seq = jnp.where(response == 1, coef, -coef)
+    ab[0] = loss_scale * mk * (2.0 * z_weight * lt - seq) * jnp.exp(st[0] - lt)
+    ab[1] = loss_scale * mk * seq
+
+    def gradient(d, s):
+        u = 2 * d + s
+        lanes = slice(s * tl, (s + 1) * tl)
+        b = jnp.where(is_label(d, s), ab[1, u : u + 1, :], 0.0)
+        g = LT[d, :, lanes] * ab[0, u : u + 1, :] + b
+        GT[d, :, lanes] = g.astype(BF16)
+        G[d, s] = g.T.astype(BF16)
+
     first, second = (1, 2), (2, 1)
 
     def cols(i):
@@ -218,42 +322,58 @@
         return jnp.dot(G[d, s], w[:, cols(i)], preferred_element_type=F32)
 
     c1, c2, cz = {}, {}, []
-
-    def send_first(i):
+    second_term, own_term = {}, {}
+
+    def send_first(i, h):
+        hs = slice(h * hr, (h + 1) * hr)
         for s in range(2):
             f = first[s]
-            S1[i, s, 1] = term(3, s, i).astype(BF16)
-            S1[i, s, 0] = term(f, s, i).astype(BF16)
-            c1[i, s] = remote(S1.at[i, s], R1.at[i, s], s1_s.at[i, s], s1_r.at[i, s], at_ctx(f))
-            c1[i, s].start()
-
-    def send_second(i):
+            if h == 0:
+                S1[i, s, 1] = term(3, s, i).astype(BF16)
+                S1[i, s, 0] = term(f, s, i).astype(BF16)
+            cp = remote(
+                S1.at[i, s, :, hs], R1.at[i, s, :, hs],
+                s1_s.at[i, s, h], s1_r.at[i, s, h], at_ctx(f),
+            )
+            cp.start()
+            c1[i, s, h] = cp
+
+    def send_second(i, h):
+        hs = slice(h * hr, (h + 1) * hr)
         for s in range(2):
             g = second[s]
-            mine = term(g, s, i)
-            c1[i, s].wait_recv()
-            S2[i, s] = (mine + R1[i, s, 1].astype(F32)).astype(BF16)
-            c2[i, s] = remote(S2.at[i, s], R2.at[i, s], s2_s.at[i, s], s2_r.at[i, s], at_ctx(g))
-            c2[i, s].start()
-
-    def send_vocab(i):
+            if h == 0:
+                second_term[s] = term(g, s, i)
+            c1[i, s, h].wait_recv()
+            S2[i, s, hs] = (second_term[s][hs] + R1[i, s, 1, hs].astype(F32)).astype(BF16)
+            cp = remote(
+                S2.at[i, s, hs], R2.at[i, s, hs], s2_s.at[i, s, h], s2_r.at[i, s, h], at_ctx(g)
+            )
+            cp.start()
+            c2[i, s, h] = cp
+
+    zm = lax.rem(z, m)
+
+    def send_vocab(i, h):
+        hs = slice(h * hr, (h + 1) * hr)
         for s in range(2):
-            mine = term(0, s, i) + R1[i, s, 0].astype(F32)
-            c2[i, s].wait_recv()
-            mine = mine + R2[i, s].astype(F32)
+            if h == 0:
+                own_term[s] = term(0, s, i)
+            mine = own_term[s][hs] + R1[i, s, 0, hs].astype(F32)
+            c2[i, s, h].wait_recv()
+            mine = mine + R2[i, s, hs].astype(F32)
             if i == PARTS - 1:
-                FA[s] = mine
-            ZS[i, s] = mine.astype(BF16)
-        zm = lax.rem(z, m)
+                FA[s, hs] = mine
+            ZS[i, s, hs] = mine.astype(BF16)
         for k in reversed(range(m)):
             x = (PARTS - 1 - i) * m + k
             if x == 0:
                 continue
             if m == 1:
-                src = ZS.at[i]
+                src = ZS.at[i, :, hs]
             else:
-                src = ZS.at[i, :, :, pl.ds(pl.multiple_of(flip(zm, k) * cw, cw), cw)]
-            cp = remote(src, ZR.at[x], z_s.at[x], z_r.at[x], at_vocab(x))
+                src = ZS.at[i, :, hs, pl.ds(pl.multiple_of(flip(zm, k) * cw, cw), cw)]
+            cp = remote(src, ZR.at[x, :, hs], z_s.at[x, h], z_r.at[x, h], at_vocab(x))
             cp.start()
             cz.append(cp)
 
@@ -278,21 +398,42 @@
 
         lax.fori_loop(low, high, body, 0)
 
-    send_first(0)
-    send_first(1)
-    head(0, head_tiles // 2)
-    send_second(0)
-    send_first(2)
-    head(head_tiles // 2, head_tiles)
-    send_second(1)
-    send_vocab(0)
-    send_first(3)
-    send_second(2)
-    send_vocab(1)
-    send_second(3)
-    send_vocab(2)
-    send_vocab(3)
-    zm = lax.rem(z, m)
+    for d, s in ((3, 0), (1, 0), (3, 1), (2, 1)):
+        gradient(d, s)
+    send_first(0, 0)
+    send_first(0, 1)
+    for d, s in ((2, 0), (1, 1), (0, 0), (0, 1)):
+        gradient(d, s)
+    send_first(1, 0)
+    head(0, 1)
+    send_second(0, 0)
+    send_first(1, 1)
+    head(1, 2)
+    send_second(0, 1)
+    send_first(2, 0)
+    head(2, 3)
+    send_second(1, 0)
+    send_vocab(0, 0)
+    send_first(2, 1)
+    head(3, 4)
+    send_second(1, 1)
+    send_vocab(0, 1)
+    send_first(3, 0)
+    head(4, 5)
+    send_second(2, 0)
+    send_vocab(1, 0)
+    send_first(3, 1)
+    head(5, 6)
+    send_second(2, 1)
+    send_vocab(1, 1)
+    head(6, 7)
+    send_second(3, 0)
+    send_vocab(2, 0)
+    head(7, head_tiles)
+    send_second(3, 1)
+    send_vocab(2, 1)
+    send_vocab(3, 0)
+    send_vocab(3, 1)
     own = pl.ds(0, cw) if m == 1 else pl.ds(pl.multiple_of(zm * cw, cw), cw)
     for cp in cz:
         cp.wait_recv()
@@ -304,8 +445,11 @@
     out = pltpu.make_async_copy(GO, gh_out, lsem.at[2])
     out.start()
     to_partner.wait_send()
-    for cp in ag + [fwd0, fwd1]:
+    for cp in ag:
         cp.wait_send()
+    for j in range(3):
+        for d in (1, 2, 3):
+            chain_wait_send(j, d)
     for cp in list(c1.values()) + list(c2.values()) + cz:
         cp.wait_send()
 
@@ -353,10 +497,11 @@
                 vm((2, tl, CW), F32),
                 vm((rows, half), BF16),
                 vm((2, tl, cw), BF16),
-                vm((4, 2, 8, tl), F32),
-                vm((4, 2, 8, tl), F32),
-                vm((n, 4, 2, 8, tl), F32),
-                vm((4, 4, 2, 8, tl), F32),
+                vm((3, 8, tl), F32),
+                vm((3, 8, tl), F32),
+                vm((n, 3, 8, tl), F32),
+                vm((4, 3, 8, tl), F32),
+                vm((2, 8, tl), F32),
                 vm((2, 8, toks), jnp.int32),
                 vm((2, 8, 128), F32),
                 dma((3,)),
@@ -364,18 +509,22 @@
                 dma((4,)),
                 dma((4, 2)),
                 dma((4, 2)),
+                dma((4, 2, 2)),
+                dma((4, 2, 2)),
+                dma((2, 3, 4)),
+                dma((2, 3, 4)),
                 dma((4,)),
                 dma((4,)),
                 dma((n,)),
                 dma((n,)),
                 dma((4,)),
                 dma((4,)),
-                dma((PARTS, 2)),
-                dma((PARTS, 2)),
-                dma((PARTS, 2)),
-                dma((PARTS, 2)),
-                dma((n,)),
-                dma((n,)),
+                dma((PARTS, 2, 2)),
+                dma((PARTS, 2, 2)),
+                dma((PARTS, 2, 2)),
+                dma((PARTS, 2, 2)),
+                dma((n, 2)),
+                dma((n, 2)),
                 dma((half // 512,)),
             ],
             compiler_params=pltpu.CompilerParams(

time: 185 us -> 162 us (0.88)
  Pallas kernels: 177 us -> 154 us
    pallas_call x1, Pallas kernels: 177 us -> 154 us  [local(): pl.pallas_call(functools.partial(kernel, n), out_shape=(jax.ShapeDtypeStr...]
where the time goes in v2:
time: 162 us
  Pallas kernels  154 us (95%)
  local copies, waits for them, and re-layouts  6.57 us (4%)
  between operations  1.93 us (1%)
    pallas_call x1, Pallas kernels, local(): pl.pallas_call(functools.partial(kernel, n), out_shape=(jax.ShapeDtypeStr...  154 us
    unnamed x2, local copies, waits for them, and re-layouts  6.57 us

profile of v2, /device:TPU:0, one launch (start us, length us, event | category | flops | bytes accessed | tf_op | source)
XLA Modules:
  0.0 162.1 jit_solution(6190903644229751466)
XLA Ops:
  1.9 153.6 %shard_map.77 = (bf16[2,128,1024]{2,1,0:T(8,128)(2,1)}, bf16[512,4096]{1,0:T(8,128)(2,1)}) custom-call(bf16[1,128,8192]{2,1,0:T(8,128)(2,1)} %hid.1, bf16[512,4096]{1,0:T(8,128)(2,1)} %w_hbm.1, s32[1,512]{1,0:T(1,128)} %lab_in.1, s32[1,512]{1,0:T(1,128)} %msk_in.1, f32[1,1]{1,0:T(1,128)} %bitcast.2.oth_in, f32[1,1]{1,0:T(1,128)} %bitcast.3.ref_in), custom_call_target="tpu_custom_call" | custom-call | flops 12884901888 | bytes 12582912 | tf_op jit(solution)/shard_map/pallas_call | solution.py:476
  155.5 1.9 %copy.12 = bf16[2,128,1024]{2,1,0:T(8,128)(2,1)} copy(bf16[2,128,1024]{2,1,0:T(8,128)(2,1)} %get-tuple-element.4) | data formatting | bytes 1048576
  157.4 4.7 %copy.13 = bf16[512,4096]{1,0:T(8,128)(2,1)} copy(bf16[512,4096]{1,0:T(8,128)(2,1)} %get-tuple-element.5) | data formatting | bytes 8388608

commit v3 on v2

--- a/solution.py
+++ b/solution.py
@@ -178,9 +178,7 @@
 
     lt_copies = []
 
-    def logits(d):
-        LT[d] = jnp.zeros((rows, 2 * tl), F32)
-
+    def add_logits(d, low, high):
         def body(k, carry):
             cols = pl.ds(pl.multiple_of(k * ktile, ktile), ktile)
             block = H[d, :, :, cols].reshape(2 * tl, ktile)
@@ -189,10 +187,14 @@
             )
             return carry
 
-        lax.fori_loop(0, half // ktile, body, 0)
+        lax.fori_loop(low // ktile, high // ktile, body, 0)
+
+    def swap_logits(d):
         cp = remote(LT.at[d], LR.at[d], lt_s.at[d], lt_r.at[d], partner)
         cp.start()
         lt_copies.append(cp)
+
+    chained = zq * PARTS
 
     base = (c * n + z) * rows
 
@@ -215,7 +217,10 @@
                 jnp.where(is_label(d, s), l, 0.0), axis=0, keepdims=True
             )
 
-    logits(0)
+    for d in range(4):
+        LT[d] = jnp.zeros((rows, 2 * tl), F32)
+    add_logits(0, 0, half)
+    swap_logits(0)
     z_wait(3, 0)
     z_wait(3, 1)
     chain_send(0, (3,))
@@ -238,15 +243,21 @@
     chain_send(2, (3,))
     rest_wait(1, 1)
     rest_wait(2, 0)
+    add_logits(1, chained, half)
+    add_logits(2, chained, half)
     chain_recv(2, (1, 2))
-    logits(1)
-    logits(2)
+    add_logits(1, 0, chained)
+    swap_logits(1)
+    add_logits(2, 0, chained)
+    swap_logits(2)
     local_stats(1)
-    local_stats(2)
     chain_recv(2, (3,))
+    add_logits(3, 0, chained)
     rest_wait(3, 0)
     rest_wait(3, 1)
-    logits(3)
+    add_logits(3, chained, half)
+    swap_logits(3)
+    local_stats(2)
     local_stats(3)
 
     zc = []
@@ -324,9 +335,9 @@
     c1, c2, cz = {}, {}, []
     second_term, own_term = {}, {}
 
-    def send_first(i, h):
+    def send_first(i, h, responses=(0, 1)):
         hs = slice(h * hr, (h + 1) * hr)
-        for s in range(2):
+        for s in responses:
             f = first[s]
             if h == 0:
                 S1[i, s, 1] = term(3, s, i).astype(BF16)
@@ -398,10 +409,14 @@
 
         lax.fori_loop(low, high, body, 0)
 
-    for d, s in ((3, 0), (1, 0), (3, 1), (2, 1)):
-        gradient(d, s)
-    send_first(0, 0)
-    send_first(0, 1)
+    gradient(3, 0)
+    gradient(1, 0)
+    send_first(0, 0, (0,))
+    send_first(0, 1, (0,))
+    gradient(3, 1)
+    gradient(2, 1)
+    send_first(0, 0, (1,))
+    send_first(0, 1, (1,))
     for d, s in ((2, 0), (1, 1), (0, 0), (0, 1)):
         gradient(d, s)
     send_first(1, 0)
@@ -461,6 +476,20 @@
     out.wait()
 
 
+def hand_over(hid_ref, head_ref, hid_out, head_out, sems):
+    rows = head_ref.shape[0]
+    count = 8
+    step = rows // count
+    copies = [pltpu.make_async_copy(hid_ref, hid_out, sems.at[count])]
+    for t in range(count):
+        part = pl.ds(t * step, step)
+        copies.append(pltpu.make_async_copy(head_ref.at[part], head_out.at[part], sems.at[t]))
+    for cp in copies:
+        cp.start()
+    for cp in copies:
+        cp.wait()
+
+
 def solution(mesh):
     n = mesh.shape["vocab"]
 
@@ -473,7 +502,7 @@
         dma = pltpu.SemaphoreType.DMA
         any_spec = pl.BlockSpec(memory_space=pl.ANY)
         vmem_spec = pl.BlockSpec(memory_space=pltpu.VMEM)
-        return pl.pallas_call(
+        results = pl.pallas_call(
             functools.partial(kernel, n),
             out_shape=(
                 jax.ShapeDtypeStruct((2, tl, cw), BF16),
@@ -537,6 +566,16 @@
             hidden, head_weight, labels, token_mask,
             other_logps.reshape(1, 1), ref_logps.reshape(1, 1),
         )
+        return pl.pallas_call(
+            hand_over,
+            out_shape=tuple(jax.ShapeDtypeStruct(r.shape, r.dtype) for r in results),
+            in_specs=[any_spec, any_spec],
+            out_specs=(any_spec, any_spec),
+            scratch_shapes=[dma((9,))],
+            cost_estimate=pl.CostEstimate(
+                flops=0, bytes_accessed=4 * rows * half, transcendentals=0
+            ),
+        )(*results)
 
     return jax.shard_map(
         local,

time: 162 us -> 296 us (1.83)
  Pallas kernels: 154 us -> 293 us
  local copies, waits for them, and re-layouts: 6.57 us -> 0 us
    pallas_call x0 -> x1, Pallas kernels: none -> 144 us  [local(): pl.pallas_call(hand_over, out_shape=tuple((jax.ShapeDtypeStruct(r.shape,...]
    unnamed x2 -> x0, local copies, waits for them, and re-layouts: 6.57 us -> none
    pallas_call x1, Pallas kernels: 154 us -> 149 us  [local(): pl.pallas_call(functools.partial(kernel, n), out_shape=(jax.ShapeDtypeStr...]
where the time goes in v3:
time: 296 us; the launch traced here: 295 us
  Pallas kernels  293 us (99%)
    pallas_call x1, Pallas kernels, local(): pl.pallas_call(functools.partial(kernel, n), out_shape=(jax.ShapeDtypeStr...  149 us
    pallas_call x1, Pallas kernels, local(): pl.pallas_call(hand_over, out_shape=tuple((jax.ShapeDtypeStruct(r.shape,...  144 us

profile of v3, /device:TPU:0, one launch (start us, length us, event | category | flops | bytes accessed | tf_op | source)
XLA Modules:
  0.0 295.5 jit_solution(2386546706470384375)
XLA Ops:
  1.9 149.3 %shard_map.77 = (bf16[2,128,1024]{2,1,0:T(8,128)(2,1)}, bf16[512,4096]{1,0:T(8,128)(2,1)}) custom-call(bf16[1,128,8192]{2,1,0:T(8,128)(2,1)} %hid.1, bf16[512,4096]{1,0:T(8,128)(2,1)} %w_hbm.1, s32[1,512]{1,0:T(1,128)} %lab_in.1, s32[1,512]{1,0:T(1,128)} %msk_in.1, f32[1,1]{1,0:T(1,128)} %bitcast.2.oth_in, f32[1,1]{1,0:T(1,128)} %bitcast.3.ref_in), custom_call_target="tpu_custom_call" | custom-call | flops 12884901888 | bytes 12582912 | tf_op jit(solution)/shard_map/pallas_call | solution.py:505
  151.2 144.1 %shard_map.78 = (bf16[2,128,1024]{2,1,0:T(8,128)(2,1)}, bf16[512,4096]{1,0:T(8,128)(2,1)}) custom-call(bf16[2,128,1024]{2,1,0:T(8,128)(2,1)} %get-tuple-element.4.hid_ref, bf16[512,4096]{1,0:T(8,128)(2,1)} %get-tuple-element.5.head_ref), custom_call_target="tpu_custom_call" | custom-call | bytes 8388608 | tf_op jit(solution)/shard_map/pallas_call | solution.py:569

commit v4 on v3

--- a/solution.py
+++ b/solution.py
@@ -25,7 +25,7 @@
 
 def kernel(
     n, hid, w_hbm, lab_in, msk_in, oth_in, ref_in, gh_out, head_out,
-    w, H, LT, LR, GT, G, S1, R1, S2, R2, ZS, ZR, FA, HO, GO, st, st2, zst, cst, ab, auxi, auxf,
+    w, HX, H, LT, LR, GT, G, S1, R1, S2, R2, ZS, ZR, FA, HO, GO, st, st2, zst, cst, ab, auxi, auxf,
     lsem, psem, aux_sem, az_s, az_r, ag_s, ag_r, ch_s, ch_r, lt_s, lt_r, zst_s, zst_r, cst_s, cst_r,
     s1_s, s1_r, s2_s, s2_r, z_s, z_r, ho_sem,
 ):
@@ -56,12 +56,14 @@
             device_id=dev, device_id_type=pl.DeviceIdType.MESH,
         )
 
-    cp_w = pltpu.make_async_copy(w_hbm, w, lsem.at[0])
-    cp_w.start()
     own_cols = pl.ds(pl.multiple_of(p * half, half), half)
     other_cols = pl.ds(pl.multiple_of(q * half, half), half)
     cp_h = pltpu.make_async_copy(hid.at[0, :, own_cols], H.at[0, p], lsem.at[1])
+    cp_x = pltpu.make_async_copy(hid.at[0, :, other_cols], HX, lsem.at[3])
+    cp_x.start()
     cp_h.start()
+    cp_w = pltpu.make_async_copy(w_hbm, w, lsem.at[0])
+    cp_w.start()
     auxi[p, 0:1, :] = lab_in[...]
     auxi[p, 1:2, :] = msk_in[...]
     auxf[p, 0:1, :] = jnp.broadcast_to(oth_in[...], (1, 128))
@@ -73,8 +75,10 @@
         pl.semaphore_signal(barrier, inc=1, device_id=dev, device_id_type=pl.DeviceIdType.MESH)
     pl.semaphore_wait(barrier, len(peers))
 
-    to_partner = remote(hid.at[0, :, other_cols], H.at[0, p], psem.at[0], psem.at[1], partner)
+    cp_x.wait()
+    to_partner = remote(HX, H.at[0, p], psem.at[0], psem.at[1], partner)
     to_partner.start()
+    cp_h.wait()
     ag = []
 
     def zcols(k):
@@ -93,18 +97,14 @@
         cp.start()
         ag.append(cp)
 
-    def own_rest(h):
-        where = pl.ds(pl.multiple_of(p * half + zq * PARTS, 128), half - zq * PARTS)
-        return hid.at[0, h * hr : (h + 1) * hr, where]
-
     def held_rest(d, s, h):
         return H.at[d, s, h * hr : (h + 1) * hr, rest]
 
-    own_z = hid.at[0, :, pl.ds(pl.multiple_of(p * half + zs * zq, 128), zq)]
+    own_z = H.at[0, p, :, zcols(zs)]
     for d in (1, 2):
         send_z(0, p, own_z, d, d)
     for d in (1, 2):
-        send_rest(0, p, own_rest(0), d, d)
+        send_rest(0, p, held_rest(0, p, 0), d, d)
     ax = [
         remote(auxi.at[p], auxi.at[p], aux_sem.at[0], aux_sem.at[1], partner),
         remote(auxf.at[p], auxf.at[p], aux_sem.at[2], aux_sem.at[3], partner),
@@ -115,7 +115,7 @@
     for d in (1, 2):
         send_z(0, q, H.at[0, q, :, zcols(zs)], d, d)
     for d in (1, 2):
-        send_rest(1, p, own_rest(1), d, d)
+        send_rest(1, p, held_rest(0, p, 1), d, d)
 
     def z_wait(d, s):
         part = H.at[d, s, :, zcols(zs)]
@@ -174,7 +174,6 @@
     z_wait(2, 0)
     chain_send(0, (1, 2))
     cp_w.wait()
-    cp_h.wait()
 
     lt_copies = []
 
@@ -476,17 +475,22 @@
     out.wait()
 
 
-def hand_over(hid_ref, head_ref, hid_out, head_out, sems):
+def hand_over(hid_ref, head_ref, hid_out, head_out, hid_v, head_v, in_sems, out_sems):
     rows = head_ref.shape[0]
     count = 8
     step = rows // count
-    copies = [pltpu.make_async_copy(hid_ref, hid_out, sems.at[count])]
+    pieces = [(hid_ref, hid_v, hid_out)]
     for t in range(count):
         part = pl.ds(t * step, step)
-        copies.append(pltpu.make_async_copy(head_ref.at[part], head_out.at[part], sems.at[t]))
-    for cp in copies:
-        cp.start()
-    for cp in copies:
+        pieces.append((head_ref.at[part], head_v.at[part], head_out.at[part]))
+    reads = [pltpu.make_async_copy(a, v, in_sems.at[t]) for t, (a, v, _) in enumerate(pieces)]
+    writes = [pltpu.make_async_copy(v, o, out_sems.at[t]) for t, (_, v, o) in enumerate(pieces)]
+    for cp in reads:
+        cp.start()
+    for cp, out in zip(reads, writes):
+        cp.wait()
+        out.start()
+    for cp in writes:
         cp.wait()
 
 
@@ -512,6 +516,7 @@
             out_specs=(any_spec, any_spec),
             scratch_shapes=[
                 vm((rows, half), BF16),
+                vm((tl, half), BF16),
                 vm((4, 2, tl, half), BF16),
                 vm((4, rows, 2 * tl), F32),
                 vm((4, rows, 2 * tl), F32),
@@ -533,7 +538,7 @@
                 vm((2, 8, tl), F32),
                 vm((2, 8, toks), jnp.int32),
                 vm((2, 8, 128), F32),
-                dma((3,)),
+                dma((4,)),
                 dma((2,)),
                 dma((4,)),
                 dma((4, 2)),
@@ -571,7 +576,8 @@
             out_shape=tuple(jax.ShapeDtypeStruct(r.shape, r.dtype) for r in results),
             in_specs=[any_spec, any_spec],
             out_specs=(any_spec, any_spec),
-            scratch_shapes=[dma((9,))],
+            scratch_shapes=[vm(r.shape, r.dtype) for r in results] + [dma((9,)), dma((9,))],
+            compiler_params=pltpu.CompilerParams(vmem_limit_bytes=24 * 1024 * 1024),
             cost_estimate=pl.CostEstimate(
                 flops=0, bytes_accessed=4 * rows * half, transcendentals=0
             ),

time: 296 us -> 158 us (0.53)
  Pallas kernels: 293 us -> 152 us
  local copies, waits for them, and re-layouts: 0 us -> 3.22 us
    pallas_call x1, Pallas kernels: 144 us -> 2.65 us  [local(): pl.pallas_call(hand_over, out_shape=tuple((jax.ShapeDtypeStruct(r.shape,...]
    unnamed x0 -> x4, local copies, waits for them, and re-layouts: none -> 3.22 us
where the time goes in v4:
time: 158 us; the launch traced here: 157 us
  Pallas kernels  152 us (96%)
  local copies, waits for them, and re-layouts  3.22 us (2%)
  between operations  2.1 us (1%)
    pallas_call x1, Pallas kernels, local(): pl.pallas_call(functools.partial(kernel, n), out_shape=(jax.ShapeDtypeStr...  149 us
    unnamed x4, local copies, waits for them, and re-layouts  3.22 us

profile of v4, /device:TPU:0, one launch (start us, length us, event | category | flops | bytes accessed | tf_op | source)
XLA Modules:
  0.0 157.4 jit_solution(10737149470590811224)
XLA Ops:
  1.9 149.4 %shard_map.77 = (bf16[2,128,1024]{2,1,0:T(8,128)(2,1)}, bf16[512,4096]{1,0:T(8,128)(2,1)}) custom-call(bf16[1,128,8192]{2,1,0:T(8,128)(2,1)} %hid.1, bf16[512,4096]{1,0:T(8,128)(2,1)} %w_hbm.1, s32[1,512]{1,0:T(1,128)} %lab_in.1, s32[1,512]{1,0:T(1,128)} %msk_in.1, f32[1,1]{1,0:T(1,128)} %bitcast.2.oth_in, f32[1,1]{1,0:T(1,128)} %bitcast.3.ref_in), custom_call_target="tpu_custom_call" | custom-call | flops 12884901888 | bytes 12582912 | tf_op jit(solution)/shard_map/pallas_call | solution.py:509
  151.3 0.0 copy-start
  151.3 2.2 %copy-done = bf16[512,4096]{1,0:T(8,128)(2,1)S(1)} copy-done((bf16[512,4096]{1,0:T(8,128)(2,1)S(1)}, bf16[512,4096]{1,0:T(8,128)(2,1)}, u32[]{:S(2)}) %copy-start) | copy-done | bytes 4194328
  153.5 0.0 copy-start.1
  153.5 1.0 copy-done.1
  154.6 2.6 %shard_map.78 = (bf16[2,128,1024]{2,1,0:T(8,128)(2,1)}, bf16[512,4096]{1,0:T(8,128)(2,1)}) custom-call(bf16[2,128,1024]{2,1,0:T(8,128)(2,1)S(1)} %copy-done.1, bf16[512,4096]{1,0:T(8,128)(2,1)S(1)} %copy-done), custom_call_target="tpu_custom_call" | custom-call | bytes 8388608 | tf_op jit(solution)/shard_map/pallas_call | solution.py:574
Async XLA Ops:
  151.3 2.2 %copy-start = (bf16[512,4096]{1,0:T(8,128)(2,1)S(1)}, bf16[512,4096]{1,0:T(8,128)(2,1)}, u32[]{:S(2)}) copy-start(bf16[512,4096]{1,0:T(8,128)(2,1)} %get-tuple-element.5.head_ref) | copy-start | bytes 12582916
  153.5 1.0 copy-start.1

commit v5 on v4

--- a/solution.py
+++ b/solution.py
@@ -577,7 +577,7 @@
             in_specs=[any_spec, any_spec],
             out_specs=(any_spec, any_spec),
             scratch_shapes=[vm(r.shape, r.dtype) for r in results] + [dma((9,)), dma((9,))],
-            compiler_params=pltpu.CompilerParams(vmem_limit_bytes=24 * 1024 * 1024),
+            compiler_params=pltpu.CompilerParams(vmem_limit_bytes=58 * 1024 * 1024),
             cost_estimate=pl.CostEstimate(
                 flops=0, bytes_accessed=4 * rows * half, transcendentals=0
             ),

time: 158 us -> 156 us (0.987)
  local copies, waits for them, and re-layouts: 3.22 us -> 0 us
  Pallas kernels: 152 us -> 154 us
    unnamed x4 -> x0, local copies, waits for them, and re-layouts: 3.22 us -> none
where the time goes in v5:
time: 156 us
  Pallas kernels  154 us (99%)
  between operations  2.09 us (1%)
    pallas_call x1, Pallas kernels, local(): pl.pallas_call(functools.partial(kernel, n), out_shape=(jax.ShapeDtypeStr...  149 us
    pallas_call x1, Pallas kernels, local(): pl.pallas_call(hand_over, out_shape=tuple((jax.ShapeDtypeStruct(r.shape,...  4.16 us

profile of v5, /device:TPU:0, one launch (start us, length us, event | category | flops | bytes accessed | tf_op | source)
XLA Modules:
  0.0 155.7 jit_solution(12849193538744648682)
XLA Ops:
  1.9 149.4 %shard_map.77 = (bf16[2,128,1024]{2,1,0:T(8,128)(2,1)}, bf16[512,4096]{1,0:T(8,128)(2,1)}) custom-call(bf16[1,128,8192]{2,1,0:T(8,128)(2,1)} %hid.1, bf16[512,4096]{1,0:T(8,128)(2,1)} %w_hbm.1, s32[1,512]{1,0:T(1,128)} %lab_in.1, s32[1,512]{1,0:T(1,128)} %msk_in.1, f32[1,1]{1,0:T(1,128)} %bitcast.2.oth_in, f32[1,1]{1,0:T(1,128)} %bitcast.3.ref_in), custom_call_target="tpu_custom_call" | custom-call | flops 12884901888 | bytes 12582912 | tf_op jit(solution)/shard_map/pallas_call | solution.py:509
  151.3 4.2 %shard_map.78 = (bf16[2,128,1024]{2,1,0:T(8,128)(2,1)}, bf16[512,4096]{1,0:T(8,128)(2,1)}) custom-call(bf16[2,128,1024]{2,1,0:T(8,128)(2,1)} %get-tuple-element.4.hid_ref, bf16[512,4096]{1,0:T(8,128)(2,1)} %get-tuple-element.5.head_ref), custom_call_target="tpu_custom_call" | custom-call | bytes 8388608 | tf_op jit(solution)/shard_map/pallas_call | solution.py:574
